TPU v7x, 128 devices: a whole 4x4x4 slice. The times are simulated.
128 devices in a mesh: wide: 32 (over x_hi, z, y), narrow: 4 (over x_lo, core).
Axes of the slice: x: 4 (x_hi: 2, x_lo: 2; x = x_hi * 2 + x_lo), y: 4, z: 4, core: 2. Of those that a mesh axis runs over, the one named last changes fastest.
Arguments:
- tokens: bfloat16 [3072, 4096], P('wide'), may hold values from -6 to 6
- expert_ids: int32 [3072, 8], P('wide'), may hold values from 0 to 63, all different within a row; in each aligned block of 96 rows (0 to 95, 96 to 191, ...) at most 16 rows name the same one
- probs: float32 [3072, 8], P('wide'), may hold values from 0.02 to 1
- w_in: bfloat16 [64, 2, 4096, 1536], P('wide', None, None, 'narrow'), may hold values from -0.09375 to 0.09375
- w_down: bfloat16 [64, 1536, 4096], P('wide', 'narrow'), may hold values from -0.15625 to 0.15625
- fresh_in: bfloat16 [2, 65536, 1536], P(None, 'wide', 'narrow'), may hold values from -0.09375 to 0.09375
- fresh_down: bfloat16 [1536, 65536], P('narrow', 'wide'), may hold values from -0.15625 to 0.15625
- refresh_slot: int32 [16], replicated, may hold values from 0 to 3, as said below
Outputs:
- mixed: bfloat16 [3072, 4096], P('wide', 'narrow')
Inputs may be any that keep to these rules, and one draw needn't show every extreme that they name: `expert_ids`: in each block of 96 rows (the rows of one index of wide), no expert is named by more than 16 choices, a bound that some block reaches; a row names 8 different experts. refresh_slot[p] lies in (p mod 2) * 2 to (p mod 2) * 2 + 1, so pair p's refreshed expert is held by index 2 * p + (p mod 2) of wide; refresh_slot[0] is 0 and the last pair's is 3.
All inputs are finite; a program needn't handle non-finite values.
Results may differ from a plain program's by a relative error of at most 0.015.
Values may be sent and summed in bfloat16 or wider, within the bound.
A program may use at most 192 MiB of HBM per device.

v0:
```python
import jax
import jax.numpy as jnp
from jax import lax
from jax.sharding import PartitionSpec as P

TOP = 8
EXP_DEV = 2


def swapped(block, axis, distance):
    count = lax.axis_size(axis)
    route = []
    for low in range(count):
        high = low | 1 << distance
        if high != low and high < count:
            route += [(low, high), (high, low)]
    return lax.ppermute(block, axis, route)


def place(flat_ids, experts, capacity):
    entries = flat_ids.shape[0]
    onehot = (flat_ids[:, None] == jnp.arange(experts, dtype=jnp.int32)[None, :]).astype(jnp.int32)
    earlier = jnp.cumsum(onehot, axis=0) - onehot
    position = jnp.sum(earlier * onehot, axis=1)
    target = flat_ids * capacity + position
    source = (
        jnp.zeros((experts * capacity,), jnp.int32)
        .at[target]
        .set(jnp.arange(entries, dtype=jnp.int32))
    )
    filled = (
        jnp.zeros((experts * capacity,), jnp.int32).at[target].set(jnp.ones((entries,), jnp.int32))
    )
    return (target, source, filled)


def regroup(fresh_in, fresh_down, parts):
    halves, half_rows, blockw = fresh_in.shape
    piece = blockw // parts
    moved_in = lax.all_to_all(
        fresh_in.reshape(halves, half_rows, parts, piece),
        "narrow",
        split_axis=2,
        concat_axis=2,
        tiled=True,
    )
    rolled_in = jnp.swapaxes(moved_in, 2, 3).reshape(halves, half_rows, blockw)
    moved_down = lax.all_to_all(
        fresh_down.reshape(parts, piece, half_rows),
        "narrow",
        split_axis=0,
        concat_axis=0,
        tiled=True,
    )
    rolled_down = jnp.swapaxes(moved_down, 0, 1).reshape(blockw, half_rows)
    other_in, other_down = swapped((rolled_in, rolled_down), "wide", 0)
    lower = lax.axis_index("wide") % 2 == 0
    full_in = jnp.concatenate(
        [jnp.where(lower, rolled_in, other_in), jnp.where(lower, other_in, rolled_in)], axis=1
    )
    full_down = jnp.concatenate(
        [jnp.where(lower, rolled_down, other_down), jnp.where(lower, other_down, rolled_down)],
        axis=1,
    )
    return (full_in, full_down)


def expert_ffn(received, w_pair, w_out):
    both = jnp.einsum("secd,egdf->gsecf", received, w_pair, preferred_element_type=jnp.float32)
    hidden = (jax.nn.silu(both[0]) * both[1]).astype(jnp.bfloat16)
    return jnp.einsum("secf,efd->secd", hidden, w_out, preferred_element_type=jnp.float32)


def on_device(tokens, expert_ids, probs, w_in, w_down, fresh_in, fresh_down, refresh_slot):
    nwide = lax.axis_size("wide")
    parts = lax.axis_size("narrow")
    wide_idx = lax.axis_index("wide")
    narrow_idx = lax.axis_index("narrow")
    rows_dev, width = tokens.shape
    experts = EXP_DEV * nwide
    capacity = max(2, (4 * rows_dev * TOP + 3 * experts - 1) // (3 * experts))
    columns = width // parts
    full_in, full_down = regroup(fresh_in, fresh_down, parts)
    wanted = lax.dynamic_index_in_dim(refresh_slot, wide_idx // 2, 0, False)
    local_slots = wide_idx % 2 * EXP_DEV + jnp.arange(EXP_DEV, dtype=jnp.int32)
    match = local_slots == wanted
    w_pair = jnp.where(match[:, None, None, None], full_in[None], w_in)
    w_out = jnp.where(match[:, None, None], full_down[None], w_down)
    target, source, filled = place(expert_ids.reshape(-1), experts, capacity)
    picked = tokens[source // TOP]
    picked = jnp.where(filled[:, None] > 0, picked, jnp.zeros_like(picked))
    received = lax.all_to_all(
        picked.reshape(nwide, EXP_DEV, capacity, width),
        "wide",
        split_axis=0,
        concat_axis=0,
        tiled=True,
    )
    partial_value = expert_ffn(received, w_pair, w_out)
    summed = lax.psum(partial_value.astype(jnp.bfloat16), "narrow").astype(jnp.float32)
    own_cols = lax.dynamic_slice_in_dim(summed, narrow_idx * columns, columns, 3).astype(
        jnp.bfloat16
    )
    returned = lax.all_to_all(own_cols, "wide", split_axis=0, concat_axis=0, tiled=True).reshape(
        experts * capacity, columns
    )
    values = returned[target].reshape(rows_dev, TOP, columns).astype(jnp.float32)
    weights = probs / jnp.sum(probs, axis=1, keepdims=True)
    mixed = jnp.sum(weights[:, :, None] * values, axis=1)
    return mixed.astype(jnp.bfloat16)


def solution(mesh):
    return jax.shard_map(
        on_device,
        mesh=mesh,
        in_specs=(
            P("wide", None),
            P("wide", None),
            P("wide", None),
            P("wide", None, None, "narrow"),
            P("wide", "narrow", None),
            P(None, "wide", "narrow"),
            P("narrow", "wide"),
            P(),
        ),
        out_specs=P("wide", "narrow"),
        check_vma=False,
    )
```

profile of v0, /device:TPU:1, one launch (start us, length us, event | category | flops | bytes accessed | tf_op | source)
XLA Modules:
  0.0 588.1 jit_solution(13237266254997704443)
XLA Ops:
  6.5 5.1 all-to-all-start
  11.6 4.8 copy.26
  16.4 4.0 copy.27
  20.6 10.3 %all-to-all-done = bf16[4,96,2048]{2,1,0:T(8,128)(2,1)S(1)} async-done(((bf16[4,96,2048]{2,1,0:T(8,128)(2,1)}), bf16[4,96,2048]{2,1,0:T(8,128)(2,1)S(1)}, u32[]{:S(2)}, u32[]{:S(2)}) %all-to-all-start) | async-done | bytes 1572896 | tf_op jit(solution)/shard_map/all_to_all | solution.py:48
  30.8 5.5 all-to-all-start.1
  38.9 3.4 scatter_custom_fusion.1
  42.3 3.4 scatter_custom_fusion
  45.8 7.8 %gather_fusion = bf16[1024,4096]{1,0:T(8,128)(2,1)} fusion(bf16[96,4096]{1,0:T(8,128)(2,1)S(1)} %copy-done, s32[1024]{0:T(1024)S(1)} %fusion.25), kind=kCustom, calls=%fused_computation | custom fusion | bytes 16781312 | tf_op jit(solution)/shard_map/gather | solution.py:90
  53.6 7.2 %broadcast_select_fusion = bf16[32,2,16,4096]{3,2,1,0:T(8,128)(2,1)} fusion(bf16[32,2,16,4096]{3,2,1,0:T(8,128)(2,1)} %bitcast.65, pred[32,2,16]{2,1,0:T(4,128)(4,1)S(1)} %broadcast_in_dim.67), kind=kLoop, calls=%fused_computation.10 | loop fusion | flops 4194304 | bytes 16778240 | tf_op jit(solution)/shard_map/jit(_where)/select_n | solution.py:91
  60.9 11.6 %all-to-all-done.1 = bf16[2,2048,4,96]{1,3,0,2:T(8,128)(2,1)} async-done(((bf16[2,2048,4,96]{1,3,0,2:T(8,128)(2,1)}), bf16[2,2048,4,96]{1,3,0,2:T(8,128)(2,1)}, u32[]{:S(2)}, u32[]{:S(2)}) %all-to-all-start.1) | async-done | bytes 3145760 | tf_op jit(solution)/shard_map/all_to_all | solution.py:40
  72.5 10.7 %all-to-all-start.2 = ((bf16[32,2,16,4096]{3,2,1,0:T(8,128)(2,1)}), bf16[32,2,16,4096]{3,2,1,0:T(8,128)(2,1)}, u32[]{:S(2)}, u32[]{:S(2)}) async-start(bf16[32,2,16,4096]{3,2,1,0:T(8,128)(2,1)} %broadcast_select_fusion), calls=%async_computation.2 | async-start | bytes 16777216 | tf_op jit(solution)/shard_map/all_to_all | solution.py:92
  83.3 6.8 %copy.28 = bf16[2,2048,96,4]{1,0,3,2:T(2,128)(2,1)} copy(bf16[2,2048,96,4]{1,2,0,3:T(8,128)(2,1)} %bitcast.6) | data formatting | bytes 6291456 | tf_op jit(solution)/shard_map/transpose | solution.py:47
  97.8 188.3 %collective-permute-done = bf16[384,2048]{1,0:T(8,128)(2,1)} collective-permute-done((bf16[384,2048]{1,0:T(8,128)(2,1)S(1)}, bf16[384,2048]{1,0:T(8,128)(2,1)}, u32[]{:S(2)}, u32[]{:S(2)}) %collective-permute-start) | collective-permute-done | bytes 1572896 | tf_op jit(solution)/shard_map/ppermute | solution.py:17
  289.7 7.3 %broadcast_select_fusion.2 = (bf16[2,2048,384]{1,0,2:T(2,128)(2,1)S(1)}, bf16[2,2048,384]{1,0,2:T(2,128)(2,1)S(1)}) fusion(bf16[2,2048,384]{1,0,2:T(2,128)(2,1)} %collective-permute-done.1, pred[]{:T(512)S(6)} %eq.47, bf16[2,2048,96,4]{1,0,3,2:T(2,128)(2,1)} %copy.28), kind=kLoop, calls=%fused_computation.17 | loop fusion | flops 3145728 | bytes 12582913 | tf_op jit(solution)/shard_map/jit(_where)/select_n | solution.py:59
  297.0 8.3 %pad_maximum_fusion = bf16[2,4096,384]{1,0,2:T(2,128)(2,1)} fusion(bf16[2,2048,384]{1,0,2:T(2,128)(2,1)S(1)} %get-tuple-element.6, bf16[2,2048,384]{1,0,2:T(2,128)(2,1)S(1)} %get-tuple-element.5), kind=kLoop, calls=%fused_computation.11 | loop fusion | flops 12582912 | bytes 12582912 | tf_op jit(solution)/shard_map/concatenate | solution.py:58
  305.3 16.4 %copy.29 = bf16[2,4096,384]{2,1,0:T(8,128)(2,1)} copy(bf16[2,4096,384]{1,0,2:T(2,128)(2,1)} %pad_maximum_fusion) | data formatting | bytes 12582912 | tf_op jit(solution)/shard_map/concatenate | solution.py:58
  321.6 22.2 %fusion.11 = f32[2,32,2,16,384]{4,1,3,0,2:T(8,128)} fusion(bf16[32,2,16,4096,1]{3,2,1,0,4:T(8,128)(2,1)} %bitcast.12, bf16[2,2,4096,384]{3,2,1,0:T(8,128)(2,1)} %param.11, pred[2]{0:T(512)(128)(4,1)S(1)} %add_compare_fusion, bf16[2,4096,384]{2,1,0:T(8,128)(2,1)} %copy.29), kind=kOutput, calls=%fused_computation.23 | convolution fusion | flops 6448742400 | bytes 30408706 | tf_op jit(solution)/shard_map/secd,egdf->gsecf/dot_general | solution.py:69
  343.8 10.6 %convert_bitcast_fusion = bf16[32,2,16,4096]{3,0,2,1:T(8,128)(2,1)} fusion(bf16[2,384,4096]{2,1,0:T(8,128)(2,1)} %param.12, pred[2]{0:T(512)(128)(4,1)S(1)} %add_compare_fusion, bf16[384,4096]{1,0:T(8,128)(2,1)} %pad_maximum_fusion.1, f32[2,32,2,16,384]{4,1,3,0,2:T(8,128)} %fusion.11), kind=kOutput, calls=%fused_computation.9 | convolution fusion | flops 3230924800 | bytes 20971522 | tf_op jit(solution)/shard_map/secf,efd->secd/dot_general | solution.py:71
  354.4 179.4 %all-reduce.2.cloned.1.call-done = bf16[32,2,16,4096]{3,0,2,1:T(8,128)(2,1)} async-done(((bf16[32,2,16,4096]{3,0,2,1:T(8,128)(2,1)}), bf16[32,2,16,4096]{3,0,2,1:T(8,128)(2,1)}) %all-reduce.2.cloned.1.call-update) | async-done | bytes 8388624 | tf_op jit(solution)/shard_map/psum | solution.py:100
  535.6 2.5 copy.36
  538.1 9.2 %all-to-all-start.3 = ((bf16[32,2,16,1024]{3,2,1,0:T(8,128)(2,1)}), bf16[32,2,16,1024]{3,2,1,0:T(8,128)(2,1)S(1)}, u32[]{:S(2)}, u32[]{:S(2)}) async-start(bf16[32,2,16,1024]{3,2,1,0:T(8,128)(2,1)} %copy.36), calls=%async_computation.3 | async-start | bytes 4194304 | tf_op jit(solution)/shard_map/all_to_all | solution.py:104
  547.5 27.0 %all-to-all-done.3 = bf16[32,2,16,1024]{3,2,1,0:T(8,128)(2,1)S(1)} async-done(((bf16[32,2,16,1024]{3,2,1,0:T(8,128)(2,1)}), bf16[32,2,16,1024]{3,2,1,0:T(8,128)(2,1)S(1)}, u32[]{:S(2)}, u32[]{:S(2)}) %all-to-all-start.3) | async-done | bytes 2097184 | tf_op jit(solution)/shard_map/all_to_all | solution.py:104
  574.5 3.6 gather_fusion.1
  578.1 3.1 fusion.9
  (44 shorter events, 16.1 us)
Async XLA Ops:
  6.5 39.3 %copy-start = (bf16[96,4096]{1,0:T(8,128)(2,1)S(1)}, bf16[96,4096]{1,0:T(8,128)(2,1)}, u32[]{:S(2)}) copy-start(bf16[96,4096]{1,0:T(8,128)(2,1)} %param.8) | copy-start | bytes 2359300
  6.5 24.3 %all-to-all-start = ((bf16[4,96,2048]{2,1,0:T(8,128)(2,1)}), bf16[4,96,2048]{2,1,0:T(8,128)(2,1)S(1)}, u32[]{:S(2)}, u32[]{:S(2)}) async-start(bf16[4,96,2048]{2,1,0:T(8,128)(2,1)} %bitcast.68), calls=%async_computation | async-start | bytes 3145728 | tf_op jit(solution)/shard_map/all_to_all | solution.py:48
  16.4 4.0 copy-start.3
  30.8 41.6 %all-to-all-start.1 = ((bf16[2,2048,4,96]{1,3,0,2:T(8,128)(2,1)}), bf16[2,2048,4,96]{1,3,0,2:T(8,128)(2,1)}, u32[]{:S(2)}, u32[]{:S(2)}) async-start(bf16[2,2048,4,96]{1,3,0,2:T(8,128)(2,1)} %copy.27), calls=%async_computation.1 | async-start | bytes 6291456 | tf_op jit(solution)/shard_map/all_to_all | solution.py:40
  72.5 249.1 %all-to-all-start.2 = ((bf16[32,2,16,4096]{3,2,1,0:T(8,128)(2,1)}), bf16[32,2,16,4096]{3,2,1,0:T(8,128)(2,1)}, u32[]{:S(2)}, u32[]{:S(2)}) async-start(bf16[32,2,16,4096]{3,2,1,0:T(8,128)(2,1)} %broadcast_select_fusion), calls=%async_computation.2 | async-start | bytes 16777216 | tf_op jit(solution)/shard_map/all_to_all | solution.py:92
  83.2 450.6 %all-reduce.2.cloned.1.call-start = ((), (), s32[]{:S(2)}) async-start(), calls=%async_computation.4 | async-start | bytes 16777216 | tf_op jit(solution)/shard_map/psum | solution.py:100
  90.1 199.6 %collective-permute-start.1 = (bf16[2,2048,384]{1,0,2:T(2,128)(2,1)}, bf16[2,2048,384]{1,0,2:T(2,128)(2,1)}, u32[]{:S(2)}, u32[]{:S(2)}) collective-permute-start(bf16[2,2048,384]{1,0,2:T(2,128)(2,1)} %bitcast.7), channel_id=1, source_target_pairs={{0,4},{4,0},{8,12},{12,8},{16,20},{20,16},{24,28},{28,24},{32,36},... | collective-permute-start | bytes 9437192 | tf_op jit(solution)/shard_map/ppermute | solution.py:17
  91.2 5.3 copy-start.4
  96.0 190.1 %collective-permute-start = (bf16[384,2048]{1,0:T(8,128)(2,1)S(1)}, bf16[384,2048]{1,0:T(8,128)(2,1)}, u32[]{:S(2)}, u32[]{:S(2)}) collective-permute-start(bf16[384,2048]{1,0:T(8,128)(2,1)S(1)} %reshape.88), channel_id=1, source_target_pairs={{0,4},{4,0},{8,12},{12,8},{16,20},{20,16},{24,28},{28,24},{32,36},... | collective-permute-start | bytes 4718600 | tf_op jit(solution)/shard_map/ppermute | solution.py:17
  538.1 9.2 %copy-start.2 = (f32[96,8]{0,1:T(8,128)S(1)}, f32[96,8]{0,1:T(8,128)}, u32[]{:S(2)}) copy-start(f32[96,8]{0,1:T(8,128)} %param.10) | copy-start | bytes 9220
  538.1 36.4 %all-to-all-start.3 = ((bf16[32,2,16,1024]{3,2,1,0:T(8,128)(2,1)}), bf16[32,2,16,1024]{3,2,1,0:T(8,128)(2,1)S(1)}, u32[]{:S(2)}, u32[]{:S(2)}) async-start(bf16[32,2,16,1024]{3,2,1,0:T(8,128)(2,1)} %copy.36), calls=%async_computation.3 | async-start | bytes 4194304 | tf_op jit(solution)/shard_map/all_to_all | solution.py:104
  574.5 6.7 %copy-start.1 = (bf16[96,4096]{1,0:T(8,128)(2,1)S(1)}, bf16[96,4096]{1,0:T(8,128)(2,1)}, u32[]{:S(2)}) copy-start(bf16[96,4096]{1,0:T(8,128)(2,1)} %param.8) | copy-start | bytes 2359300
Sparse Core Ops, SparseCore 0:
  354.5 179.2 all-reduce.1
where the time goes:
time: 590 us; the launch traced here: 588 us
  waiting for transfers between devices  417 us (71%)
  local copies, waits for them, and re-layouts  58.8 us (10%)
  other arithmetic  34 us (6%)
  matrix products  32.7 us (6%)
  starting transfers between devices  32.3 us (5%)
  between operations  13.6 us (2%)
    ppermute x2, waiting for transfers between devices, swapped(): return lax.ppermute(block, axis, route)  188 us
    psum x1, waiting for transfers between devices, on_device(): lax.psum(partial_value.astype(jnp.bfloat16), 'narrow').astype(jnp.float32)  179 us
    all_to_all x1, waiting for transfers between devices, on_device(): lax.all_to_all(own_cols, 'wide', split_axis=0, concat_axis=0, tiled=True)  27 us
    dot_general x1, matrix products, expert_ffn(): jnp.einsum('secd,egdf->gsecf', received, w_pair, preferred_element_type=j...  22.2 us
    concatenate x1, local copies, waits for them, and re-layouts, regroup(): jnp.concatenate([jnp.where(lower, rolled_in, other_in), jnp.where(lower,...  16.4 us
  transfers between devices with their start and end apart: 7, of which 5 were waited for; matrix products, arithmetic and copies ran while one was open for 14% of the time, Pallas kernels for 0%

commit v1 on v0

v1 whole, which is shorter than its diff:
```python
import functools

import jax
import jax.numpy as jnp
from jax import lax
from jax.experimental import pallas as pl
from jax.experimental.pallas import tpu as pltpu
from jax.sharding import PartitionSpec as P

MESH = pl.DeviceIdType.MESH
CAP = 16
BF16 = jnp.bfloat16
F32 = jnp.float32


def dot(a, b):
    return jnp.dot(a, b, preferred_element_type=F32)


def routing(ids, probs, slots, sel_ref, coef_ref):
    rows, top = ids.shape
    count = sel_ref.shape[1]
    experts = count // CAP
    pairs = experts // 4
    q = lax.broadcasted_iota(jnp.int32, (1, experts), 1)
    kind, pair = q // pairs, q % pairs
    fresh = jnp.zeros((1, experts), jnp.int32)
    for p in range(pairs):
        fresh = jnp.where(pair == p, slots[p], fresh)
    odd = pair % 2
    kept = 4 * pair + 2 - 2 * odd
    expert = jnp.where(
        kind < 2, kept + kind, jnp.where(kind == 2, 4 * pair + 4 * odd + 1 - fresh, 4 * pair + fresh)
    )
    names = jnp.zeros((rows, experts), F32)
    weight = jnp.zeros((rows, experts), F32)
    for k in range(top):
        hit = ids[:, k : k + 1] == expert
        names = jnp.where(hit, 1.0, names)
        weight = jnp.where(hit, probs[:, k : k + 1], weight)
    weight = weight / jnp.sum(probs, axis=1, keepdims=True)
    later = lax.broadcasted_iota(jnp.int32, (rows, rows), 0)
    earlier = lax.broadcasted_iota(jnp.int32, (rows, rows), 1)
    before = jnp.where(earlier < later, 1.0, 0.0).astype(BF16)
    position = dot(before, names.astype(BF16))
    key = jnp.where(names > 0.0, position, -1.0).astype(BF16)
    column = lax.broadcasted_iota(jnp.int32, (experts, count), 1)
    spread = jnp.where(
        column // CAP == lax.broadcasted_iota(jnp.int32, (experts, count), 0), 1.0, 0.0
    ).astype(BF16)
    slot = (lax.broadcasted_iota(jnp.int32, (rows, count), 1) % CAP).astype(F32)
    sel = jnp.where(dot(key, spread) == slot, 1.0, 0.0)
    sel_ref[...] = sel.astype(BF16)
    high = weight.astype(BF16)
    low = (weight - high.astype(F32)).astype(BF16)
    coef_ref[:rows] = (sel * dot(high, spread)).astype(BF16)
    coef_ref[rows:] = (sel * dot(low, spread)).astype(BF16)


def gated(gate, up):
    return (gate / (1.0 + jnp.exp(-gate)) * up).astype(BF16)


def kernel(
    nwide,
    tok_hbm,
    ids_ref,
    probs_ref,
    slot_ref,
    wi_hbm,
    wd_hbm,
    fi_hbm,
    fd_hbm,
    out_ref,
    tok,
    sel,
    coef,
    picked,
    recv_r,
    recv_k,
    wi,
    wd,
    fi,
    fd,
    acc,
    hid,
    hid_r,
    part_out,
    part_in,
    in_r,
    in_k,
    ret,
    mix_out,
    mix_in,
    load_sem,
    dsend,
    drecv,
    fsend,
    frecv,
    osend,
    orecv,
    psend,
    precv,
    rsend,
    rrecv,
):
    rows, wblk = out_ref.shape
    total = nwide * CAP
    half = total // 2
    npair = nwide // 2
    per_kind = npair * CAP
    tile = wblk // 2
    wide, narrow = lax.axis_index("wide"), lax.axis_index("narrow")
    x_hi = wide // (nwide // 2)
    x_lo, core = narrow // 2, narrow % 2
    pair, side = wide // 2, wide % 2
    pair_odd = pair % 2
    owner = 1 - (side + pair_odd) % 2
    sibling = (wide, x_lo * 2 + 1 - core)
    mate = (wide, (1 - x_lo) * 2 + core)
    partner = (pair * 2 + 1 - side, narrow)

    def peer(index):
        other = (x_lo + x_hi + index // (nwide // 2)) % 2
        return (index, other * 2 + core)

    def remote(src, dst, send, recv, device):
        return pltpu.make_async_remote_copy(
            src_ref=src, dst_ref=dst, send_sem=send, recv_sem=recv, device_id=device, device_id_type=MESH
        )

    def arrived(ref, sem):
        pltpu.make_async_copy(ref, ref, sem).wait()

    def block(ref, index):
        return ref.at[pl.ds(pl.multiple_of(index * CAP, CAP), CAP)]

    loads = [
        pltpu.make_async_copy(
            tok_hbm.at[:, pl.ds(pl.multiple_of(core * wblk, wblk), wblk)], tok.at[:, :wblk], load_sem.at[0]
        ),
        pltpu.make_async_copy(
            tok_hbm.at[:, pl.ds(pl.multiple_of((core + 2) * wblk, wblk), wblk)],
            tok.at[:, wblk:],
            load_sem.at[1],
        ),
        pltpu.make_async_copy(fi_hbm, fi, load_sem.at[2]),
        pltpu.make_async_copy(fd_hbm, fd, load_sem.at[3]),
        pltpu.make_async_copy(wi_hbm, wi, load_sem.at[4]),
        pltpu.make_async_copy(wd_hbm, wd, load_sem.at[5]),
    ]
    for load in loads:
        load.start()

    barrier = pltpu.get_barrier_semaphore()

    def greet(i, carry):
        pl.semaphore_signal(
            barrier, inc=1, device_id=peer((wide + i) % nwide), device_id_type=MESH
        )
        return carry

    lax.fori_loop(1, nwide, greet, 0)
    pl.semaphore_signal(barrier, inc=1, device_id=sibling, device_id_type=MESH)
    pl.semaphore_signal(barrier, inc=1, device_id=mate, device_id_type=MESH)

    routing(ids_ref[...], probs_ref[...], slot_ref, sel, coef)
    loads[0].wait()
    loads[1].wait()

    def pick(kind):
        span = pl.ds(kind * per_kind, per_kind)
        picked[span, :] = lax.dot_general(
            sel[:, span], tok[...], (((0,), (0,)), ((), ())), preferred_element_type=F32
        ).astype(BF16)

    pick(3)
    pl.semaphore_wait(barrier, nwide + 1)

    def piece_r(index):
        return picked.at[
            pl.ds(pl.multiple_of(3 * per_kind + index // 2 * CAP, CAP), CAP),
            pl.ds(pl.multiple_of(index % 2 * wblk, wblk), wblk),
        ]

    def send_r(i, carry):
        index = (wide + i) % nwide
        remote(
            piece_r(index), block(recv_r.at[core], wide), dsend.at[2], drecv.at[2], peer(index)
        ).start()
        return carry

    lax.fori_loop(1, nwide, send_r, 0)
    pltpu.make_async_copy(piece_r(wide), block(recv_r.at[core], wide), drecv.at[2]).start()

    pick(0)
    pick(2)

    def piece_0(index):
        to_owner = 1 - (index % 2 + index // 2) % 2
        return picked.at[
            pl.ds(pl.multiple_of(to_owner * (2 * per_kind) + index // 2 * CAP, CAP), CAP)
        ]

    def send_0(i, carry):
        index = (wide + i) % nwide
        remote(
            piece_0(index), block(recv_k.at[0, core], wide), dsend.at[0], drecv.at[0], peer(index)
        ).start()
        return carry

    lax.fori_loop(1, nwide, send_0, 0)
    pltpu.make_async_copy(piece_0(wide), block(recv_k.at[0, core], wide), drecv.at[0]).start()

    pick(1)

    def piece_1(index):
        return picked.at[pl.ds(pl.multiple_of(per_kind + index * CAP, CAP), CAP)]

    def send_1(i, carry):
        to_pair = (pair + i) % npair
        index = 2 * to_pair + 1 - to_pair % 2

        @pl.when(index != wide)
        def _():
            remote(
                piece_1(to_pair),
                block(recv_k.at[1, core], wide),
                dsend.at[1],
                drecv.at[1],
                peer(index),
            ).start()

        return carry

    lax.fori_loop(0, npair, send_1, 0)

    @pl.when(owner == 0)
    def _():
        pltpu.make_async_copy(piece_1(pair), block(recv_k.at[1, core], wide), drecv.at[1]).start()

    mine = pl.ds(pl.multiple_of(side * half, half), half)
    theirs = pl.ds(pl.multiple_of((1 - side) * half, half), half)
    arrived(recv_r.at[core], drecv.at[2])
    forward = remote(recv_r.at[core], recv_r.at[core], fsend.at[2], frecv.at[2], sibling)
    forward.start()
    loads[2].wait()
    depth = pl.ds(pl.multiple_of(core * wblk, wblk), wblk)
    for g in range(2):
        acc[g] = dot(recv_r[core], fi[g, depth, :])
    arrived(recv_r.at[1 - core], frecv.at[2])
    depth = pl.ds(pl.multiple_of((1 - core) * wblk, wblk), wblk)
    for g in range(2):
        acc[g] += dot(recv_r[1 - core], fi[g, depth, :])
    for g in range(2):
        part_out[g] = acc[g, theirs, :].astype(BF16)
    swap = remote(part_out, part_in, psend.at[0], precv.at[0], partner)
    swap.start()
    loads[3].wait()
    swap.wait_recv()
    hid_r[mine, :] = gated(
        acc[0, mine, :] + part_in[0].astype(F32), acc[1, mine, :] + part_in[1].astype(F32)
    )
    share = remote(hid_r.at[mine], hid_r.at[mine], psend.at[1], precv.at[1], partner)
    share.start()
    forward.wait_send()
    arrived(hid_r.at[theirs], precv.at[1])
    given = []
    for t in range(2):
        span = pl.ds(t * tile, tile)
        columns = pl.ds(pl.multiple_of((1 - core) * wblk + t * tile, tile), tile)
        recv_r[1 - core, :, span] = dot(hid_r[...], fd[:, columns]).astype(BF16)
        copy = remote(
            recv_r.at[1 - core, :, span], in_r.at[:, span], osend.at[2, t], orecv.at[2, t], sibling
        )
        copy.start()
        given.append(copy)
    for t in range(2):
        span = pl.ds(t * tile, tile)
        columns = pl.ds(pl.multiple_of(core * wblk + t * tile, tile), tile)
        given[t].wait_recv()
        recv_r[core, :, span] = (
            dot(hid_r[...], fd[:, columns]) + in_r[:, span].astype(F32)
        ).astype(BF16)

    def slot_r():
        return ret.at[
            pl.ds(pl.multiple_of(3 * per_kind + pair * CAP, CAP), CAP),
            pl.ds(pl.multiple_of(side * wblk, wblk), wblk),
        ]

    def back_r(i, carry):
        index = (wide + i) % nwide
        remote(
            block(recv_r.at[core], index), slot_r(), rsend.at[2], rrecv.at[3], peer(index)
        ).start()
        return carry

    lax.fori_loop(1, nwide, back_r, 0)
    pltpu.make_async_copy(block(recv_r.at[core], wide), slot_r(), rrecv.at[3]).start()

    loads[4].wait()
    loads[5].wait()
    unchanged = (slot_ref[pair] + 1) % 2

    def one_expert(i, carry):
        expert = jnp.where(owner == 1, unchanged, i)
        kind = owner * 2 + (1 - owner) * i
        arrived(recv_k.at[i, core], drecv.at[i])
        forward = remote(recv_k.at[i, core], recv_k.at[i, core], fsend.at[i], frecv.at[i], sibling)
        forward.start()
        for b in range(2):
            depth = pl.ds(pl.multiple_of((core + 2 * b) * wblk, wblk), wblk)
            for g in range(2):
                part = dot(recv_k[i, core, :, b * wblk : (b + 1) * wblk], wi[expert, g, depth, :])
                if b == 0:
                    acc[g] = part
                else:
                    acc[g] += part
        arrived(recv_k.at[i, 1 - core], frecv.at[i])
        for b in range(2):
            depth = pl.ds(pl.multiple_of((1 - core + 2 * b) * wblk, wblk), wblk)
            for g in range(2):
                acc[g] += dot(
                    recv_k[i, 1 - core, :, b * wblk : (b + 1) * wblk], wi[expert, g, depth, :]
                )
        hid[...] = gated(acc[0], acc[1])
        forward.wait_send()
        given = []
        for t in range(4):
            span = pl.ds(t * tile, tile)
            first = (1 - core + t // 2 * 2) * wblk + t % 2 * tile
            columns = pl.ds(pl.multiple_of(first, tile), tile)
            recv_k[i, 1 - core, :, span] = dot(hid[...], wd[expert, :, columns]).astype(BF16)
            copy = remote(
                recv_k.at[i, 1 - core, :, span],
                in_k.at[i, :, span],
                osend.at[i, t],
                orecv.at[i, t],
                sibling,
            )
            copy.start()
            given.append(copy)
        for t in range(4):
            span = pl.ds(t * tile, tile)
            first = (core + t // 2 * 2) * wblk + t % 2 * tile
            columns = pl.ds(pl.multiple_of(first, tile), tile)
            given[t].wait_recv()
            recv_k[i, core, :, span] = (
                dot(hid[...], wd[expert, :, columns]) + in_k[i, :, span].astype(F32)
            ).astype(BF16)

        slot = ret.at[pl.ds(pl.multiple_of(kind * per_kind + pair * CAP, CAP), CAP)]

        def back(j, inner):
            index = (wide + j) % nwide
            remote(
                block(recv_k.at[i, core], index), slot, rsend.at[i], rrecv.at[kind], peer(index)
            ).start()
            return inner

        lax.fori_loop(1, nwide, back, 0)
        pltpu.make_async_copy(block(recv_k.at[i, core], wide), slot, rrecv.at[kind]).start()
        for t in range(4):
            given[t].wait_send()
        return carry

    lax.fori_loop(0, 2 - owner, one_expert, 0)

    for kind in (3, 0, 2, 1):
        arrived(ret.at[pl.ds(kind * per_kind, per_kind)], rrecv.at[kind])

    def mixed(which):
        both = dot(coef[...], ret[:, pl.ds(pl.multiple_of(which * wblk, wblk), wblk)])
        return both[:rows] + both[rows:]

    mix_out[...] = mixed(1 - x_lo).astype(BF16)
    last = remote(mix_out, mix_in, psend.at[2], precv.at[2], mate)
    last.start()
    own = mixed(x_lo)
    last.wait_recv()
    out_ref[...] = (own + mix_in[...].astype(F32)).astype(BF16)

    swap.wait_send()
    share.wait_send()
    last.wait_send()
    for copy in given:
        copy.wait_send()
    sent = total - CAP
    arrived(recv_r.at[0, pl.ds(0, sent)], dsend.at[2])
    arrived(recv_r.at[0, pl.ds(0, sent)], rsend.at[2])
    arrived(recv_k.at[0, 0, pl.ds(0, sent)], dsend.at[0])
    arrived(recv_k.at[0, 0, pl.ds(0, sent)], rsend.at[0])

    @pl.when(owner == 1)
    def _():
        arrived(recv_k.at[0, 0, pl.ds(0, per_kind)], dsend.at[1])

    @pl.when(owner == 0)
    def _():
        arrived(recv_k.at[0, 0, pl.ds(0, per_kind - CAP)], dsend.at[1])
        arrived(recv_k.at[0, 0, pl.ds(0, sent)], rsend.at[1])


def on_device(nwide, tokens, expert_ids, probs, w_in, w_down, fresh_in, fresh_down, refresh_slot):
    rows, width = tokens.shape
    units = w_down.shape[1]
    wblk = width // 4
    total = nwide * CAP
    slots = 2 * total
    dma = pltpu.SemaphoreType.DMA
    hbm = pl.BlockSpec(memory_space=pl.ANY)
    vmem = pl.BlockSpec(memory_space=pltpu.VMEM)
    return pl.pallas_call(
        functools.partial(kernel, nwide),
        out_shape=jax.ShapeDtypeStruct((rows, wblk), BF16),
        in_specs=[hbm, vmem, vmem, pl.BlockSpec(memory_space=pltpu.SMEM), hbm, hbm, hbm, hbm],
        out_specs=vmem,
        scratch_shapes=[
            pltpu.VMEM((rows, 2 * wblk), BF16),
            pltpu.VMEM((rows, slots), BF16),
            pltpu.VMEM((2 * rows, slots), BF16),
            pltpu.VMEM((slots, 2 * wblk), BF16),
            pltpu.VMEM((2, total, wblk), BF16),
            pltpu.VMEM((2, 2, total, 2 * wblk), BF16),
            pltpu.VMEM(w_in.shape, BF16),
            pltpu.VMEM(w_down.shape, BF16),
            pltpu.VMEM(fresh_in.shape, BF16),
            pltpu.VMEM(fresh_down.shape, BF16),
            pltpu.VMEM((2, total, units), F32),
            pltpu.VMEM((total, units), BF16),
            pltpu.VMEM((total, units), BF16),
            pltpu.VMEM((2, total // 2, units), BF16),
            pltpu.VMEM((2, total // 2, units), BF16),
            pltpu.VMEM((total, wblk), BF16),
            pltpu.VMEM((2, total, 2 * wblk), BF16),
            pltpu.VMEM((slots, 2 * wblk), BF16),
            pltpu.VMEM((rows, wblk), BF16),
            pltpu.VMEM((rows, wblk), BF16),
            dma((6,)),
            dma((3,)),
            dma((3,)),
            dma((3,)),
            dma((3,)),
            dma((3, 4)),
            dma((3, 4)),
            dma((3,)),
            dma((3,)),
            dma((3,)),
            dma((4,)),
        ],
        compiler_params=pltpu.CompilerParams(
            collective_id=0, has_side_effects=True, vmem_limit_bytes=63 * 1024 * 1024
        ),
    )(tokens, expert_ids, probs, refresh_slot, w_in, w_down, fresh_in, fresh_down)


def solution(mesh):
    return jax.shard_map(
        functools.partial(on_device, mesh.shape["wide"]),
        mesh=mesh,
        in_specs=(
            P("wide", None),
            P("wide", None),
            P("wide", None),
            P("wide", None, None, "narrow"),
            P("wide", "narrow", None),
            P(None, "wide", "narrow"),
            P("narrow", "wide"),
            P(),
        ),
        out_specs=P("wide", "narrow"),
        check_vma=False,
    )
```

time: 590 us -> 175 us (0.30)
  waiting for transfers between devices: 417 us -> 0 us
  Pallas kernels: 0 us -> 169 us
  local copies, waits for them, and re-layouts: 58.8 us -> 4.41 us
  other arithmetic: 34 us -> 0 us
  matrix products: 32.7 us -> 0 us
  starting transfers between devices: 32.3 us -> 0 us
  between operations: 13.6 us -> 0.01 us
    ppermute x2 -> x0, waiting for transfers between devices: 188 us -> none  [swapped(): return lax.ppermute(block, axis, route)]
    psum x1 -> x0, waiting for transfers between devices: 179 us -> none  [on_device(): lax.psum(partial_value.astype(jnp.bfloat16), 'narrow').astype(jnp.float32)]
    pallas_call x0 -> x1, Pallas kernels: none -> 169 us  [on_device(): pl.pallas_call(functools.partial(kernel, nwide), out_shape=jax.ShapeDtype...]
    all_to_all x4 -> x0, waiting for transfers between devices: 48.9 us -> none  [the longest x1 27 us: on_device(): lax.all_to_all(own_cols, 'wide', split_axis=0, concat_axis=0, tiled=True)]
    dot_general x2 -> x0, matrix products: 32.7 us -> none  [the longest x1 22.2 us: expert_ffn(): jnp.einsum('secd,egdf->gsecf', received, w_pair, preferred_element_type=j...]
    all_to_all x4 -> x0, starting transfers between devices: 30.5 us -> none  [the longest x1 10.7 us: on_device(): lax.all_to_all(picked.reshape(nwide, EXP_DEV, capacity, width), 'wide', s...]
    concatenate x1 -> x0, local copies, waits for them, and re-layouts: 16.4 us -> none  [regroup(): jnp.concatenate([jnp.where(lower, rolled_in, other_in), jnp.where(lower,...]
    select_n x4 -> x0, other arithmetic: 16.2 us -> none  [the longest x1 7.3 us: regroup(): jnp.where(lower, rolled_in, other_in)]
  transfers between devices with their start and end apart: 7 -> 0, of which waited for: 5 -> 0; matrix products, arithmetic and copies ran while one was open for 14% -> 0% of each run, Pallas kernels for 0% -> 0%
where the time goes in v1:
time: 175 us; the launch traced here: 173 us
  Pallas kernels  169 us (97%)
  local copies, waits for them, and re-layouts  4.41 us (3%)
    pallas_call x1, Pallas kernels, on_device(): pl.pallas_call(functools.partial(kernel, nwide), out_shape=jax.ShapeDtype...  169 us
    unnamed x3, local copies, waits for them, and re-layouts  4.41 us

profile of v1, /device:TPU:1, one launch (start us, length us, event | category | flops | bytes accessed | tf_op | source)
XLA Modules:
  0.0 173.3 jit_solution(9991911627965579501)
XLA Ops:
  0.0 1.4 copy.9.ids_ref
  1.4 1.4 copy.10.probs_ref
  2.8 168.9 %shard_map.82 = bf16[96,1024]{1,0:T(8,128)(2,1)} custom-call(bf16[96,4096]{1,0:T(8,128)(2,1)} %tok_hbm.1, s32[96,8]{1,0:T(8,128)} %copy.9.ids_ref, f32[96,8]{1,0:T(8,128)} %copy.10.probs_ref, s32[16]{0:T(128)} %slot_ref.1, bf16[2,2,4096,384]{3,2,1,0:T(8,128)(2,1)} %wi_hbm.1, bf16[2,384,4096]{2,1,0:T(8,128)(2,1)} %wd_hbm.1, bf16[2,2048,384]{2,1,0:T(8,128)(2,1)} %fi_hbm.1, ...), custom_call_target="tpu_custom_call" | custom-call | tf_op jit(solution)/shard_map/pallas_call | solution.py:414
  171.7 1.6 copy.12

commit v2 on v1

v2 whole, which is shorter than its diff:
```python
import functools

import jax
import jax.numpy as jnp
from jax import lax
from jax.experimental import pallas as pl
from jax.experimental.pallas import tpu as pltpu
from jax.sharding import PartitionSpec as P

MESH = pl.DeviceIdType.MESH
CAP = 16
GROUPS = 4
BF16 = jnp.bfloat16
F32 = jnp.float32


def dot(a, b):
    return jnp.dot(a, b, preferred_element_type=F32)


def routing(ids, probs, slots):
    top, rows = ids.shape
    pairs = slots.shape[0]
    experts = 4 * pairs
    q = lax.broadcasted_iota(jnp.int32, (experts, 1), 0)
    kind, pair = q // pairs, q % pairs
    fresh = jnp.zeros((experts, 1), jnp.int32)
    for p in range(pairs):
        fresh = jnp.where(pair == p, slots[p], fresh)
    odd = pair % 2
    kept = 4 * pair + 2 - 2 * odd
    expert = jnp.where(
        kind < 2, kept + kind, jnp.where(kind == 2, 4 * pair + 4 * odd + 1 - fresh, 4 * pair + fresh)
    )
    names = jnp.zeros((experts, rows), F32)
    weight = jnp.zeros((experts, rows), F32)
    for k in range(top):
        hit = ids[k : k + 1] == expert
        names = jnp.where(hit, 1.0, names)
        weight = jnp.where(hit, probs[k : k + 1], weight)
    weight = weight / jnp.sum(probs, axis=0, keepdims=True)
    earlier = lax.broadcasted_iota(jnp.int32, (rows, rows), 0)
    later = lax.broadcasted_iota(jnp.int32, (rows, rows), 1)
    before = jnp.where(earlier < later, 1.0, 0.0).astype(BF16)
    position = dot(names.astype(BF16), before)
    return jnp.where(names > 0.0, position, -1.0).astype(BF16), weight


def spread(kind, pairs):
    row = lax.broadcasted_iota(jnp.int32, (pairs * CAP, 4 * pairs), 0)
    column = lax.broadcasted_iota(jnp.int32, (pairs * CAP, 4 * pairs), 1)
    return jnp.where(row // CAP + kind * pairs == column, 1.0, 0.0).astype(BF16)


def gated(gate, up):
    return (gate / (1.0 + jnp.exp(-gate)) * up).astype(BF16)


def kernel(
    nwide,
    tok_hbm,
    ids_ref,
    probs_ref,
    slot_ref,
    wi_hbm,
    wd_hbm,
    fi_hbm,
    fd_hbm,
    out_ref,
    tok,
    sel,
    coef,
    picked,
    recv_r,
    recv_k,
    wi,
    wd,
    fi,
    fd,
    acc,
    hid,
    hid_r,
    part_out,
    part_in,
    part_own,
    in_r,
    in_k,
    ret,
    mix_out,
    mix_in,
    load_sem,
    dsend,
    drecv,
    fsend,
    frecv,
    csend,
    crecv,
    osend,
    orecv,
    psend,
    precv,
    rsend,
    rrecv,
):
    rows, wblk = out_ref.shape
    total = nwide * CAP
    half = total // 2
    npair = nwide // 2
    per_kind = npair * CAP
    tile = wblk // 2
    lone = 3 * wblk // 4
    direct = 2 * wblk - lone
    common = wblk - lone
    group = nwide // GROUPS
    span_g = group * CAP
    wide, narrow = lax.axis_index("wide"), lax.axis_index("narrow")
    x_hi = wide // (nwide // 2)
    x_lo, core = narrow // 2, narrow % 2
    pair, side = wide // 2, wide % 2
    pair_odd = pair % 2
    owner = 1 - (side + pair_odd) % 2
    sibling = (wide, x_lo * 2 + 1 - core)
    mate = (wide, (1 - x_lo) * 2 + core)
    partner = (pair * 2 + 1 - side, narrow)

    def peer(index):
        other = (x_lo + x_hi + index // (nwide // 2)) % 2
        return (index, other * 2 + core)

    def turn(i, sign=1):
        plane, step = nwide // 2, i // 2
        if plane == 16:
            z = wide // 4 % 4 + 4 + sign * ((step + step // 4) % 4)
            y = wide % 4 + 4 + sign * (step % 4)
            spot = z % 4 * 4 + y % 4
        else:
            spot = (wide + plane + sign * step) % plane
        return (x_hi + i) % 2 * plane + spot

    def remote(src, dst, send, recv, device):
        return pltpu.make_async_remote_copy(
            src_ref=src, dst_ref=dst, send_sem=send, recv_sem=recv, device_id=device, device_id_type=MESH
        )

    def arrived(ref, sem):
        pltpu.make_async_copy(ref, ref, sem).wait()

    def across(which):
        return pl.ds(pl.multiple_of(which * lone, 128), direct)

    def alone(which):
        return pl.ds(pl.multiple_of(which * direct, 128), lone)

    def block(ref, index):
        return ref.at[pl.ds(pl.multiple_of(index * CAP, CAP), CAP)]

    loads = [
        pltpu.make_async_copy(
            tok_hbm.at[:, pl.ds(pl.multiple_of(core * wblk, wblk), wblk)], tok.at[:, :wblk], load_sem.at[0]
        ),
        pltpu.make_async_copy(
            tok_hbm.at[:, pl.ds(pl.multiple_of((core + 2) * wblk, wblk), wblk)],
            tok.at[:, wblk:],
            load_sem.at[1],
        ),
        pltpu.make_async_copy(fi_hbm, fi, load_sem.at[2]),
        pltpu.make_async_copy(fd_hbm, fd, load_sem.at[3]),
        pltpu.make_async_copy(wi_hbm, wi, load_sem.at[4]),
        pltpu.make_async_copy(wd_hbm, wd, load_sem.at[5]),
    ]
    for load in loads:
        load.start()

    barrier = pltpu.get_barrier_semaphore()

    def greet(i, carry):
        pl.semaphore_signal(
            barrier, inc=1, device_id=peer(turn(i)), device_id_type=MESH
        )
        return carry

    lax.fori_loop(1, nwide, greet, 0)
    pl.semaphore_signal(barrier, inc=1, device_id=sibling, device_id_type=MESH)
    pl.semaphore_signal(barrier, inc=1, device_id=mate, device_id_type=MESH)

    key, weight = routing(ids_ref[...], probs_ref[...], slot_ref)
    loads[0].wait()
    loads[1].wait()

    def pick(kind):
        span = pl.ds(kind * per_kind, per_kind)
        slot = lax.broadcasted_iota(jnp.int32, (per_kind, rows), 0) % CAP
        chosen = jnp.where(dot(spread(kind, npair), key) == slot.astype(F32), 1.0, 0.0).astype(BF16)
        sel[span, :] = chosen
        picked[span, :] = dot(chosen, tok[...]).astype(BF16)

    pick(3)
    pl.semaphore_wait(barrier, nwide + 1)

    def piece_r(index):
        return picked.at[
            pl.ds(pl.multiple_of(3 * per_kind + index // 2 * CAP, CAP), CAP),
            pl.ds(pl.multiple_of(index % 2 * wblk, wblk), wblk),
        ]

    def send_r(i, carry):
        index = turn(i)
        remote(
            piece_r(index), block(recv_r.at[core], wide), dsend.at[2], drecv.at[2, 0], peer(index)
        ).start()
        return carry

    lax.fori_loop(1, nwide, send_r, 0)
    pltpu.make_async_copy(piece_r(wide), block(recv_r.at[core], wide), drecv.at[2, 0]).start()

    pick(0)
    pick(2)

    def send_kept(i, which, row):
        index = turn(i)
        device = peer(index)
        columns = across(device[1] // 2)
        remote(
            picked.at[pl.ds(pl.multiple_of(row(index), CAP), CAP), columns],
            block(recv_k.at[which, core], i).at[:, columns],
            dsend.at[which],
            drecv.at[which, i // group],
            device,
        ).start()

    def keep_kept(which, row):
        columns = across(x_lo)
        pltpu.make_async_copy(
            picked.at[pl.ds(pl.multiple_of(row(wide), CAP), CAP), columns],
            block(recv_k.at[which, core], 0).at[:, columns],
            drecv.at[which, 0],
        ).start()

    def row_0(index):
        to_owner = 1 - (index % 2 + index // 2) % 2
        return to_owner * (2 * per_kind) + index // 2 * CAP

    def send_0(i, carry):
        send_kept(i, 0, row_0)
        return carry

    lax.fori_loop(1, nwide, send_0, 0)
    keep_kept(0, row_0)

    pick(1)

    def row_1(index):
        return per_kind + index // 2 * CAP

    def send_1(i, carry):
        index = turn(i)

        @pl.when((index % 2 + index // 2) % 2 == 1)
        def _():
            send_kept(i, 1, row_1)

        return carry

    lax.fori_loop(1, nwide, send_1, 0)

    @pl.when(owner == 0)
    def _():
        keep_kept(1, row_1)

    high = weight.astype(BF16)
    low = (weight - high.astype(F32)).astype(BF16)
    for part, value in enumerate((high, low)):
        for kind in range(4):
            span = pl.ds(kind * per_kind, per_kind)
            taken = sel[span, :].astype(F32) * dot(spread(kind, npair), value)
            coef[part * rows : (part + 1) * rows, span] = taken.T.astype(BF16)

    mine = pl.ds(pl.multiple_of(side * half, half), half)
    theirs = pl.ds(pl.multiple_of((1 - side) * half, half), half)
    forward = remote(recv_r.at[core], recv_r.at[core], fsend.at[2, 0, 0], frecv.at[2, 0, 0], sibling)
    swap = remote(part_out, part_in, psend.at[0], precv.at[0], partner)
    share = remote(hid_r.at[mine], hid_r.at[mine], psend.at[1], precv.at[1], partner)

    def fresh_partial():
        arrived(recv_r.at[core], drecv.at[2, 0])
        forward.start()
        loads[2].wait()
        depth = pl.ds(pl.multiple_of(core * wblk, wblk), wblk)
        for g in range(2):
            acc[g] = dot(recv_r[core], fi[g, depth, :])
        forward.wait_recv()
        depth = pl.ds(pl.multiple_of((1 - core) * wblk, wblk), wblk)
        for g in range(2):
            acc[g] += dot(recv_r[1 - core], fi[g, depth, :])
        for g in range(2):
            part_out[g] = acc[g, theirs, :].astype(BF16)
            part_own[g] = acc[g, mine, :]
        swap.start()

    def fresh_hidden():
        swap.wait_recv()
        hid_r[mine, :] = gated(
            part_own[0] + part_in[0].astype(F32), part_own[1] + part_in[1].astype(F32)
        )
        share.start()

    def give(which, t, source, target, span):
        return remote(
            source.at[:, span], target.at[:, span], osend.at[which, t], orecv.at[which, t], sibling
        )

    def fresh_down_and_back():
        loads[3].wait()
        forward.wait_send()
        arrived(hid_r.at[theirs], precv.at[1])
        given = []
        for t in range(2):
            span = pl.ds(t * tile, tile)
            columns = pl.ds(pl.multiple_of((1 - core) * wblk + t * tile, tile), tile)
            recv_r[1 - core, :, span] = dot(hid_r[...], fd[:, columns]).astype(BF16)
            given.append(give(2, t, recv_r.at[1 - core], in_r, span))
            given[t].start()
        for t in range(2):
            span = pl.ds(t * tile, tile)
            columns = pl.ds(pl.multiple_of(core * wblk + t * tile, tile), tile)
            given[t].wait_recv()
            recv_r[core, :, span] = (
                dot(hid_r[...], fd[:, columns]) + in_r[:, span].astype(F32)
            ).astype(BF16)
        slot = ret.at[
            pl.ds(pl.multiple_of(3 * per_kind + pair * CAP, CAP), CAP),
            pl.ds(pl.multiple_of(side * wblk, wblk), wblk),
        ]

        def back(i, carry):
            index = turn(i)
            remote(
                block(recv_r.at[core], index), slot, rsend.at[2], rrecv.at[3], peer(index)
            ).start()
            return carry

        lax.fori_loop(1, nwide, back, 0)
        pltpu.make_async_copy(block(recv_r.at[core], wide), slot, rrecv.at[3]).start()
        for copy in given:
            copy.wait_send()

    unchanged = (slot_ref[pair] + 1) % 2
    near, far = across(x_lo), alone(1 - x_lo)

    def rows_of(which, g, columns, where=core):
        return recv_k.at[which, where, pl.ds(g * span_g, span_g), columns]

    def forward_near(which, g):
        ref = rows_of(which, g, near)
        return remote(ref, ref, fsend.at[which, g, 0], frecv.at[which, g, 0], sibling)

    def forward_far(which, g):
        ref = rows_of(which, g, far)
        return remote(ref, ref, fsend.at[which, g, 1], frecv.at[which, g, 1], sibling)

    def lend(which, g):
        ref = rows_of(which, g, alone(x_lo))
        return remote(ref, ref, csend.at[which, g], crecv.at[which, g], mate)

    def relay(which, g):
        if g < GROUPS:
            arrived(rows_of(which, g, near), drecv.at[which, g])
            lend(which, g).start()
            forward_near(which, g).start()
        if g > 0:
            arrived(rows_of(which, g - 1, far), crecv.at[which, g - 1])
            forward_far(which, g - 1).start()

    def gate_and_up(which, expert):
        def multiply(where, offset, row, size, first=False):
            offset, row = pl.multiple_of(offset, 128), pl.multiple_of(row, 128)
            for g in range(2):
                part = dot(
                    recv_k[which, where, :, pl.ds(offset, size)], wi[expert, g, pl.ds(row, size), :]
                )
                if first:
                    acc[g] = part
                else:
                    acc[g] += part

        def multiply_alone(where, chip, first=False):
            row = (where + 2 * chip) * wblk + chip * common
            multiply(where, chip * direct, row, lone, first)

        def multiply_common(where):
            multiply(where, lone, where * wblk + lone, common)
            multiply(where, wblk, (where + 2) * wblk, common)

        multiply_alone(core, x_lo, True)
        multiply_common(core)
        multiply_alone(core, 1 - x_lo)
        for g in range(GROUPS):
            forward_near(which, g).wait_recv()
        multiply_alone(1 - core, x_lo)
        multiply_common(1 - core)
        for g in range(GROUPS):
            forward_far(which, g).wait_recv()
        multiply_alone(1 - core, 1 - x_lo)
        hid[...] = gated(acc[0], acc[1])

    def down_and_back(which, expert, kind):
        for g in range(GROUPS):
            lend(which, g).wait_send()
            forward_near(which, g).wait_send()
            forward_far(which, g).wait_send()
        given = []
        for t in range(4):
            span = pl.ds(t * tile, tile)
            first = (1 - core + t // 2 * 2) * wblk + t % 2 * tile
            columns = pl.ds(pl.multiple_of(first, tile), tile)
            recv_k[which, 1 - core, :, span] = dot(hid[...], wd[expert, :, columns]).astype(BF16)
            given.append(give(which, t, recv_k.at[which, 1 - core], in_k.at[which], span))
            given[t].start()
        for t in range(4):
            span = pl.ds(t * tile, tile)
            first = (core + t // 2 * 2) * wblk + t % 2 * tile
            columns = pl.ds(pl.multiple_of(first, tile), tile)
            given[t].wait_recv()
            recv_k[which, core, :, span] = (
                dot(hid[...], wd[expert, :, columns]) + in_k[which, :, span].astype(F32)
            ).astype(BF16)
        slot = ret.at[pl.ds(pl.multiple_of(kind * per_kind + pair * CAP, CAP), CAP)]

        def back(i, carry):
            remote(
                block(recv_k.at[which, core], i),
                slot,
                rsend.at[which],
                rrecv.at[kind],
                peer(turn(i, -1)),
            ).start()
            return carry

        lax.fori_loop(1, nwide, back, 0)
        pltpu.make_async_copy(block(recv_k.at[which, core], 0), slot, rrecv.at[kind]).start()
        for copy in given:
            copy.wait_send()

    first_expert = owner * unchanged
    fresh_partial()
    for g in range(GROUPS + 1):
        relay(0, g)
    loads[4].wait()
    loads[5].wait()
    gate_and_up(0, first_expert)
    fresh_hidden()

    @pl.when(owner == 0)
    def _():
        relay(1, 0)

    down_and_back(0, first_expert, owner * 2)

    @pl.when(owner == 0)
    def _():
        relay(1, 1)
        relay(1, 2)

    fresh_down_and_back()

    @pl.when(owner == 0)
    def _():
        for g in range(3, GROUPS + 1):
            relay(1, g)
        gate_and_up(1, 1)
        down_and_back(1, 1, 1)

    for kind in (0, 2, 3, 1):
        arrived(ret.at[pl.ds(kind * per_kind, per_kind)], rrecv.at[kind])

    def mixed(which):
        both = dot(coef[...], ret[:, pl.ds(pl.multiple_of(which * wblk, wblk), wblk)])
        return both[:rows] + both[rows:]

    mix_out[...] = mixed(1 - x_lo).astype(BF16)
    last = remote(mix_out, mix_in, psend.at[2], precv.at[2], mate)
    last.start()
    own = mixed(x_lo)
    last.wait_recv()
    out_ref[...] = (own + mix_in[...].astype(F32)).astype(BF16)

    swap.wait_send()
    share.wait_send()
    last.wait_send()
    sent = total - CAP
    arrived(recv_r.at[0, pl.ds(0, sent)], dsend.at[2])
    arrived(recv_r.at[0, pl.ds(0, sent)], rsend.at[2])
    arrived(recv_k.at[0, 0, pl.ds(0, sent), :direct], dsend.at[0])
    arrived(recv_k.at[0, 0, pl.ds(0, sent)], rsend.at[0])

    @pl.when(owner == 1)
    def _():
        arrived(recv_k.at[0, 0, pl.ds(0, per_kind), :direct], dsend.at[1])

    @pl.when(owner == 0)
    def _():
        arrived(recv_k.at[0, 0, pl.ds(0, per_kind - CAP), :direct], dsend.at[1])
        arrived(recv_k.at[0, 0, pl.ds(0, sent)], rsend.at[1])


def on_device(nwide, tokens, expert_ids, probs, w_in, w_down, fresh_in, fresh_down, refresh_slot):
    rows, width = tokens.shape
    units = w_down.shape[1]
    wblk = width // 4
    total = nwide * CAP
    slots = 2 * total
    dma = pltpu.SemaphoreType.DMA
    hbm = pl.BlockSpec(memory_space=pl.ANY)
    vmem = pl.BlockSpec(memory_space=pltpu.VMEM)
    return pl.pallas_call(
        functools.partial(kernel, nwide),
        out_shape=jax.ShapeDtypeStruct((rows, wblk), BF16),
        in_specs=[hbm, vmem, vmem, pl.BlockSpec(memory_space=pltpu.SMEM), hbm, hbm, hbm, hbm],
        out_specs=vmem,
        scratch_shapes=[
            pltpu.VMEM((rows, 2 * wblk), BF16),
            pltpu.VMEM((slots, rows), BF16),
            pltpu.VMEM((2 * rows, slots), BF16),
            pltpu.VMEM((slots, 2 * wblk), BF16),
            pltpu.VMEM((2, total, wblk), BF16),
            pltpu.VMEM((2, 2, total, 2 * wblk), BF16),
            pltpu.VMEM(w_in.shape, BF16),
            pltpu.VMEM(w_down.shape, BF16),
            pltpu.VMEM(fresh_in.shape, BF16),
            pltpu.VMEM(fresh_down.shape, BF16),
            pltpu.VMEM((2, total, units), F32),
            pltpu.VMEM((total, units), BF16),
            pltpu.VMEM((total, units), BF16),
            pltpu.VMEM((2, total // 2, units), BF16),
            pltpu.VMEM((2, total // 2, units), BF16),
            pltpu.VMEM((2, total // 2, units), F32),
            pltpu.VMEM((total, wblk), BF16),
            pltpu.VMEM((2, total, 2 * wblk), BF16),
            pltpu.VMEM((slots, 2 * wblk), BF16),
            pltpu.VMEM((rows, wblk), BF16),
            pltpu.VMEM((rows, wblk), BF16),
            dma((6,)),
            dma((3,)),
            dma((3, GROUPS)),
            dma((3, GROUPS, 2)),
            dma((3, GROUPS, 2)),
            dma((2, GROUPS)),
            dma((2, GROUPS)),
            dma((3, 4)),
            dma((3, 4)),
            dma((3,)),
            dma((3,)),
            dma((3,)),
            dma((4,)),
        ],
        compiler_params=pltpu.CompilerParams(
            collective_id=0, has_side_effects=True, vmem_limit_bytes=63 * 1024 * 1024
        ),
    )(tokens, expert_ids.T, probs.T, refresh_slot, w_in, w_down, fresh_in, fresh_down)


def solution(mesh):
    return jax.shard_map(
        functools.partial(on_device, mesh.shape["wide"]),
        mesh=mesh,
        in_specs=(
            P("wide", None),
            P("wide", None),
            P("wide", None),
            P("wide", None, None, "narrow"),
            P("wide", "narrow", None),
            P(None, "wide", "narrow"),
            P("narrow", "wide"),
            P(),
        ),
        out_specs=P("wide", "narrow"),
        check_vma=False,
    )
```

time: 175 us -> 137 us (0.78); the launches traced: 173 us -> 137 us
  Pallas kernels: 169 us -> 135 us
  local copies, waits for them, and re-layouts: 4.41 us -> 1.62 us
    pallas_call x1, Pallas kernels: 169 us -> 135 us  [on_device(): pl.pallas_call(functools.partial(kernel, nwide), out_shape=jax.ShapeDtype...]
    unnamed x3 -> x1, local copies, waits for them, and re-layouts: 4.41 us -> 1.62 us
where the time goes in v2:
time: 137 us
  Pallas kernels  135 us (99%)
  local copies, waits for them, and re-layouts  1.62 us (1%)
    pallas_call x1, Pallas kernels, on_device(): pl.pallas_call(functools.partial(kernel, nwide), out_shape=jax.ShapeDtype...  135 us

profile of v2, /device:TPU:1, one launch (start us, length us, event | category | flops | bytes accessed | tf_op | source)
XLA Modules:
  0.0 137.1 jit_solution(3515248089675010228)
XLA Ops:
  0.0 135.5 %shard_map.82 = bf16[96,1024]{1,0:T(8,128)(2,1)} custom-call(bf16[96,4096]{1,0:T(8,128)(2,1)} %tok_hbm.1, s32[8,96]{1,0:T(8,128)} %bitcast.2, f32[8,96]{1,0:T(8,128)} %bitcast.3, s32[16]{0:T(128)} %slot_ref.1, bf16[2,2,4096,384]{3,2,1,0:T(8,128)(2,1)} %wi_hbm.1, bf16[2,384,4096]{2,1,0:T(8,128)(2,1)} %wd_hbm.1, bf16[2,2048,384]{2,1,0:T(8,128)(2,1)} %fi_hbm.1, ...), custom_call_target="tpu_custom_call" | custom-call | tf_op jit(solution)/shard_map/pallas_call | solution.py:515
  135.5 1.6 %copy.10 = bf16[96,1024]{1,0:T(8,128)(2,1)} copy(bf16[96,1024]{1,0:T(8,128)(2,1)} %shard_map.82) | data formatting | bytes 393216

commit v3 on v2

--- a/solution.py
+++ b/solution.py
@@ -85,7 +85,9 @@
     part_own,
     in_r,
     in_k,
+    in_x,
     ret,
+    mixing,
     mix_out,
     mix_in,
     load_sem,
@@ -95,6 +97,8 @@
     frecv,
     csend,
     crecv,
+    xsend,
+    xrecv,
     osend,
     orecv,
     psend,
@@ -171,6 +175,9 @@
     for load in loads:
         load.start()
 
+    for blank in (pl.ds(0, lone), pl.ds(direct, lone)):
+        ret[: 3 * per_kind, blank] = jnp.zeros((3 * per_kind, lone), BF16)
+
     barrier = pltpu.get_barrier_semaphore()
 
     def greet(i, carry):
@@ -194,32 +201,17 @@
         sel[span, :] = chosen
         picked[span, :] = dot(chosen, tok[...]).astype(BF16)
 
-    pick(3)
-    pl.semaphore_wait(barrier, nwide + 1)
-
-    def piece_r(index):
-        return picked.at[
-            pl.ds(pl.multiple_of(3 * per_kind + index // 2 * CAP, CAP), CAP),
-            pl.ds(pl.multiple_of(index % 2 * wblk, wblk), wblk),
-        ]
-
-    def send_r(i, carry):
-        index = turn(i)
-        remote(
-            piece_r(index), block(recv_r.at[core], wide), dsend.at[2], drecv.at[2, 0], peer(index)
-        ).start()
-        return carry
-
-    lax.fori_loop(1, nwide, send_r, 0)
-    pltpu.make_async_copy(piece_r(wide), block(recv_r.at[core], wide), drecv.at[2, 0]).start()
-
     pick(0)
     pick(2)
+    pl.semaphore_wait(barrier, nwide + 1)
+
+    def incoming(which, chip):
+        return across(chip) if which == 0 else pl.ds(0, 2 * wblk)
 
     def send_kept(i, which, row):
         index = turn(i)
         device = peer(index)
-        columns = across(device[1] // 2)
+        columns = incoming(which, device[1] // 2)
         remote(
             picked.at[pl.ds(pl.multiple_of(row(index), CAP), CAP), columns],
             block(recv_k.at[which, core], i).at[:, columns],
@@ -229,7 +221,7 @@
         ).start()
 
     def keep_kept(which, row):
-        columns = across(x_lo)
+        columns = incoming(which, x_lo)
         pltpu.make_async_copy(
             picked.at[pl.ds(pl.multiple_of(row(wide), CAP), CAP), columns],
             block(recv_k.at[which, core], 0).at[:, columns],
@@ -246,6 +238,24 @@
 
     lax.fori_loop(1, nwide, send_0, 0)
     keep_kept(0, row_0)
+
+    pick(3)
+
+    def piece_r(index):
+        return picked.at[
+            pl.ds(pl.multiple_of(3 * per_kind + index // 2 * CAP, CAP), CAP),
+            pl.ds(pl.multiple_of(index % 2 * wblk, wblk), wblk),
+        ]
+
+    def send_r(i, carry):
+        index = turn(i)
+        remote(
+            piece_r(index), block(recv_r.at[core], wide), dsend.at[2], drecv.at[2, 0], peer(index)
+        ).start()
+        return carry
+
+    lax.fori_loop(1, nwide, send_r, 0)
+    pltpu.make_async_copy(piece_r(wide), block(recv_r.at[core], wide), drecv.at[2, 0]).start()
 
     pick(1)
 
@@ -345,13 +355,13 @@
             copy.wait_send()
 
     unchanged = (slot_ref[pair] + 1) % 2
-    near, far = across(x_lo), alone(1 - x_lo)
+    far = alone(1 - x_lo)
 
     def rows_of(which, g, columns, where=core):
         return recv_k.at[which, where, pl.ds(g * span_g, span_g), columns]
 
     def forward_near(which, g):
-        ref = rows_of(which, g, near)
+        ref = rows_of(which, g, incoming(which, x_lo))
         return remote(ref, ref, fsend.at[which, g, 0], frecv.at[which, g, 0], sibling)
 
     def forward_far(which, g):
@@ -364,12 +374,19 @@
 
     def relay(which, g):
         if g < GROUPS:
-            arrived(rows_of(which, g, near), drecv.at[which, g])
-            lend(which, g).start()
+            arrived(rows_of(which, g, incoming(which, x_lo)), drecv.at[which, g])
+            if which == 0:
+                lend(which, g).start()
             forward_near(which, g).start()
-        if g > 0:
+        if g > 0 and which == 0:
             arrived(rows_of(which, g - 1, far), crecv.at[which, g - 1])
             forward_far(which, g - 1).start()
+
+    def alone_at(where, chip):
+        return chip * direct, (where + 2 * chip) * wblk + chip * common
+
+    def common_at(where):
+        return (lone, where * wblk + lone), (wblk, (where + 2) * wblk)
 
     def gate_and_up(which, expert):
         def multiply(where, offset, row, size, first=False):
@@ -384,51 +401,55 @@
                     acc[g] += part
 
         def multiply_alone(where, chip, first=False):
-            row = (where + 2 * chip) * wblk + chip * common
-            multiply(where, chip * direct, row, lone, first)
+            multiply(where, *alone_at(where, chip), lone, first)
 
         def multiply_common(where):
-            multiply(where, lone, where * wblk + lone, common)
-            multiply(where, wblk, (where + 2) * wblk, common)
-
-        multiply_alone(core, x_lo, True)
-        multiply_common(core)
-        multiply_alone(core, 1 - x_lo)
+            for place in common_at(where):
+                multiply(where, *place, common)
+
+        if which == 0:
+            multiply_alone(core, x_lo, True)
+            multiply_common(core)
+            multiply_alone(core, 1 - x_lo)
+        else:
+            multiply(core, 0, core * wblk, wblk, True)
+            multiply(core, wblk, (core + 2) * wblk, wblk)
         for g in range(GROUPS):
             forward_near(which, g).wait_recv()
-        multiply_alone(1 - core, x_lo)
-        multiply_common(1 - core)
-        for g in range(GROUPS):
-            forward_far(which, g).wait_recv()
-        multiply_alone(1 - core, 1 - x_lo)
+        if which == 0:
+            multiply_alone(1 - core, x_lo)
+            multiply_common(1 - core)
+            for g in range(GROUPS):
+                forward_far(which, g).wait_recv()
+            multiply_alone(1 - core, 1 - x_lo)
+        else:
+            multiply(1 - core, 0, (1 - core) * wblk, wblk)
+            multiply(1 - core, wblk, (3 - core) * wblk, wblk)
         hid[...] = gated(acc[0], acc[1])
 
-    def down_and_back(which, expert, kind):
-        for g in range(GROUPS):
-            lend(which, g).wait_send()
-            forward_near(which, g).wait_send()
-            forward_far(which, g).wait_send()
-        given = []
-        for t in range(4):
-            span = pl.ds(t * tile, tile)
-            first = (1 - core + t // 2 * 2) * wblk + t % 2 * tile
-            columns = pl.ds(pl.multiple_of(first, tile), tile)
-            recv_k[which, 1 - core, :, span] = dot(hid[...], wd[expert, :, columns]).astype(BF16)
-            given.append(give(which, t, recv_k.at[which, 1 - core], in_k.at[which], span))
-            given[t].start()
-        for t in range(4):
-            span = pl.ds(t * tile, tile)
-            first = (core + t // 2 * 2) * wblk + t % 2 * tile
-            columns = pl.ds(pl.multiple_of(first, tile), tile)
-            given[t].wait_recv()
-            recv_k[which, core, :, span] = (
-                dot(hid[...], wd[expert, :, columns]) + in_k[which, :, span].astype(F32)
-            ).astype(BF16)
-        slot = ret.at[pl.ds(pl.multiple_of(kind * per_kind + pair * CAP, CAP), CAP)]
+    def tiles_at(where):
+        return (
+            (*alone_at(where, 1 - x_lo), lone),
+            (*alone_at(where, x_lo), lone),
+            *((*place, common) for place in common_at(where)),
+        )
+
+    def give_tile(which, t):
+        offset, _, size = tiles_at(core)[t]
+        span = pl.ds(pl.multiple_of(offset, 128), size)
+        return give(which, t, recv_k.at[which, 1 - core], in_k.at[which], span)
+
+    def cross(which):
+        return remote(
+            recv_k.at[which, core, :, far], in_x.at[which], xsend.at[which], xrecv.at[which], mate
+        )
+
+    def send_back(which, kind, columns):
+        slot = ret.at[pl.ds(pl.multiple_of(kind * per_kind + pair * CAP, CAP), CAP), columns]
 
         def back(i, carry):
             remote(
-                block(recv_k.at[which, core], i),
+                block(recv_k.at[which, core], i).at[:, columns],
                 slot,
                 rsend.at[which],
                 rrecv.at[kind],
@@ -437,52 +458,97 @@
             return carry
 
         lax.fori_loop(1, nwide, back, 0)
-        pltpu.make_async_copy(block(recv_k.at[which, core], 0), slot, rrecv.at[kind]).start()
-        for copy in given:
-            copy.wait_send()
+        pltpu.make_async_copy(
+            block(recv_k.at[which, core], 0).at[:, columns], slot, rrecv.at[kind]
+        ).start()
+
+    def down(which, expert, kind):
+        for g in range(GROUPS):
+            forward_near(which, g).wait_send()
+            if which == 0:
+                lend(which, g).wait_send()
+                forward_far(which, g).wait_send()
+        for t, (offset, column, size) in enumerate(tiles_at(1 - core)):
+            span = pl.ds(pl.multiple_of(offset, 128), size)
+            columns = pl.ds(pl.multiple_of(column, 128), size)
+            recv_k[which, 1 - core, :, span] = dot(hid[...], wd[expert, :, columns]).astype(BF16)
+            give_tile(which, t).start()
+
+        def own_tile(t):
+            offset, column, size = tiles_at(core)[t]
+            span = pl.ds(pl.multiple_of(offset, 128), size)
+            columns = pl.ds(pl.multiple_of(column, 128), size)
+            give_tile(which, t).wait_recv()
+            recv_k[which, core, :, span] = (
+                dot(hid[...], wd[expert, :, columns]) + in_k[which, :, span].astype(F32)
+            ).astype(BF16)
+
+        own_tile(0)
+        cross(which).start()
+        own_tile(2)
+        own_tile(3)
+        send_back(which, kind, pl.ds(lone, 2 * common))
+        own_tile(1)
+
+    def finish(which, kind):
+        cross(which).wait_recv()
+        lot = alone(x_lo)
+        recv_k[which, core, :, lot] = (
+            recv_k[which, core, :, lot].astype(F32) + in_x[which].astype(F32)
+        ).astype(BF16)
+        send_back(which, kind, lot)
+        cross(which).wait_send()
+        for t in range(4):
+            give_tile(which, t).wait_send()
 
     first_expert = owner * unchanged
-    fresh_partial()
     for g in range(GROUPS + 1):
         relay(0, g)
     loads[4].wait()
     loads[5].wait()
     gate_and_up(0, first_expert)
-    fresh_hidden()
+    down(0, first_expert, owner * 2)
+    fresh_partial()
 
     @pl.when(owner == 0)
     def _():
         relay(1, 0)
-
-    down_and_back(0, first_expert, owner * 2)
+        relay(1, 1)
+
+    finish(0, owner * 2)
 
     @pl.when(owner == 0)
     def _():
-        relay(1, 1)
-        relay(1, 2)
-
+        for g in range(2, GROUPS):
+            relay(1, g)
+        gate_and_up(1, 1)
+        down(1, 1, 1)
+
+    fresh_hidden()
     fresh_down_and_back()
 
     @pl.when(owner == 0)
     def _():
-        for g in range(3, GROUPS + 1):
-            relay(1, g)
-        gate_and_up(1, 1)
-        down_and_back(1, 1, 1)
+        finish(1, 1)
 
     for kind in (0, 2, 3, 1):
-        arrived(ret.at[pl.ds(kind * per_kind, per_kind)], rrecv.at[kind])
-
-    def mixed(which):
-        both = dot(coef[...], ret[:, pl.ds(pl.multiple_of(which * wblk, wblk), wblk)])
-        return both[:rows] + both[rows:]
-
-    mix_out[...] = mixed(1 - x_lo).astype(BF16)
+        span = pl.ds(kind * per_kind, per_kind)
+        if kind == 3:
+            arrived(ret.at[span], rrecv.at[kind])
+        else:
+            arrived(ret.at[span, across(x_lo)], rrecv.at[kind])
+        for chip in range(2):
+            columns = pl.ds(pl.multiple_of((x_lo + 1 - chip) % 2 * wblk, wblk), wblk)
+            both = dot(coef[:, span], ret[span, columns])
+            if kind == 0:
+                mixing[chip] = both[:rows] + both[rows:]
+            else:
+                mixing[chip] += both[:rows] + both[rows:]
+    mix_out[...] = mixing[0].astype(BF16)
     last = remote(mix_out, mix_in, psend.at[2], precv.at[2], mate)
     last.start()
-    own = mixed(x_lo)
     last.wait_recv()
-    out_ref[...] = (own + mix_in[...].astype(F32)).astype(BF16)
+    out_ref[...] = (mixing[1] + mix_in[...].astype(F32)).astype(BF16)
 
     swap.wait_send()
     share.wait_send()
@@ -491,16 +557,16 @@
     arrived(recv_r.at[0, pl.ds(0, sent)], dsend.at[2])
     arrived(recv_r.at[0, pl.ds(0, sent)], rsend.at[2])
     arrived(recv_k.at[0, 0, pl.ds(0, sent), :direct], dsend.at[0])
-    arrived(recv_k.at[0, 0, pl.ds(0, sent)], rsend.at[0])
+    arrived(recv_k.at[0, 0, pl.ds(0, sent), :direct], rsend.at[0])
 
     @pl.when(owner == 1)
     def _():
-        arrived(recv_k.at[0, 0, pl.ds(0, per_kind), :direct], dsend.at[1])
+        arrived(recv_k.at[0, 0, pl.ds(0, per_kind)], dsend.at[1])
 
     @pl.when(owner == 0)
     def _():
-        arrived(recv_k.at[0, 0, pl.ds(0, per_kind - CAP), :direct], dsend.at[1])
-        arrived(recv_k.at[0, 0, pl.ds(0, sent)], rsend.at[1])
+        arrived(recv_k.at[0, 0, pl.ds(0, per_kind - CAP)], dsend.at[1])
+        arrived(recv_k.at[0, 0, pl.ds(0, sent), :direct], rsend.at[1])
 
 
 def on_device(nwide, tokens, expert_ids, probs, w_in, w_down, fresh_in, fresh_down, refresh_slot):
@@ -536,7 +602,9 @@
             pltpu.VMEM((2, total // 2, units), F32),
             pltpu.VMEM((total, wblk), BF16),
             pltpu.VMEM((2, total, 2 * wblk), BF16),
+            pltpu.VMEM((2, total, wblk * 3 // 4), BF16),
             pltpu.VMEM((slots, 2 * wblk), BF16),
+            pltpu.VMEM((2, rows, wblk), F32),
             pltpu.VMEM((rows, wblk), BF16),
             pltpu.VMEM((rows, wblk), BF16),
             dma((6,)),
@@ -546,6 +614,8 @@
             dma((3, GROUPS, 2)),
             dma((2, GROUPS)),
             dma((2, GROUPS)),
+            dma((2,)),
+            dma((2,)),
             dma((3, 4)),
             dma((3, 4)),
             dma((3,)),

time: 137 us -> 123 us (0.90)
  Pallas kernels: 135 us -> 121 us
    pallas_call x1, Pallas kernels: 135 us -> 121 us  [on_device(): pl.pallas_call(functools.partial(kernel, nwide), out_shape=jax.ShapeDtype...]
where the time goes in v3:
time: 123 us; the launch traced here: 122 us
  Pallas kernels  121 us (98%)
  local copies, waits for them, and re-layouts  1.62 us (1%)
    pallas_call x1, Pallas kernels, on_device(): pl.pallas_call(functools.partial(kernel, nwide), out_shape=jax.ShapeDtype...  121 us

profile of v3, /device:TPU:1, one launch (start us, length us, event | category | flops | bytes accessed | tf_op | source)
XLA Modules:
  0.0 122.1 jit_solution(9234089764980277054)
XLA Ops:
  0.0 120.5 %shard_map.82 = bf16[96,1024]{1,0:T(8,128)(2,1)} custom-call(bf16[96,4096]{1,0:T(8,128)(2,1)} %tok_hbm.1, s32[8,96]{1,0:T(8,128)} %bitcast.2, f32[8,96]{1,0:T(8,128)} %bitcast.3, s32[16]{0:T(128)} %slot_ref.1, bf16[2,2,4096,384]{3,2,1,0:T(8,128)(2,1)} %wi_hbm.1, bf16[2,384,4096]{2,1,0:T(8,128)(2,1)} %wd_hbm.1, bf16[2,2048,384]{2,1,0:T(8,128)(2,1)} %fi_hbm.1, ...), custom_call_target="tpu_custom_call" | custom-call | tf_op jit(solution)/shard_map/pallas_call | solution.py:581
  120.5 1.6 %copy.10 = bf16[96,1024]{1,0:T(8,128)(2,1)} copy(bf16[96,1024]{1,0:T(8,128)(2,1)} %shard_map.82) | data formatting | bytes 393216

commit v4 on v3

--- a/solution.py
+++ b/solution.py
@@ -10,6 +10,7 @@
 MESH = pl.DeviceIdType.MESH
 CAP = 16
 GROUPS = 4
+HALVES = 2
 BF16 = jnp.bfloat16
 F32 = jnp.float32
 
@@ -112,7 +113,7 @@
     npair = nwide // 2
     per_kind = npair * CAP
     tile = wblk // 2
-    lone = 3 * wblk // 4
+    lone = 7 * wblk // 8
     direct = 2 * wblk - lone
     common = wblk - lone
     group = nwide // GROUPS
@@ -314,9 +315,13 @@
         )
         share.start()
 
-    def give(which, t, source, target, span):
+    def give(which, part, t, source, target, span):
         return remote(
-            source.at[:, span], target.at[:, span], osend.at[which, t], orecv.at[which, t], sibling
+            source.at[:, span],
+            target.at[:, span],
+            osend.at[which, part, t],
+            orecv.at[which, part, t],
+            sibling,
         )
 
     def fresh_down_and_back():
@@ -328,7 +333,7 @@
             span = pl.ds(t * tile, tile)
             columns = pl.ds(pl.multiple_of((1 - core) * wblk + t * tile, tile), tile)
             recv_r[1 - core, :, span] = dot(hid_r[...], fd[:, columns]).astype(BF16)
-            given.append(give(2, t, recv_r.at[1 - core], in_r, span))
+            given.append(give(2, 0, t, recv_r.at[1 - core], in_r, span))
             given[t].start()
         for t in range(2):
             span = pl.ds(t * tile, tile)
@@ -373,14 +378,14 @@
         return remote(ref, ref, csend.at[which, g], crecv.at[which, g], mate)
 
     def relay(which, g):
-        if g < GROUPS:
-            arrived(rows_of(which, g, incoming(which, x_lo)), drecv.at[which, g])
-            if which == 0:
-                lend(which, g).start()
-            forward_near(which, g).start()
-        if g > 0 and which == 0:
-            arrived(rows_of(which, g - 1, far), crecv.at[which, g - 1])
-            forward_far(which, g - 1).start()
+        arrived(rows_of(which, g, incoming(which, x_lo)), drecv.at[which, g])
+        if which == 0:
+            lend(which, g).start()
+        forward_near(which, g).start()
+
+    def relay_far(which, g):
+        arrived(rows_of(which, g, far), crecv.at[which, g])
+        forward_far(which, g).start()
 
     def alone_at(where, chip):
         return chip * direct, (where + 2 * chip) * wblk + chip * common
@@ -388,17 +393,26 @@
     def common_at(where):
         return (lone, where * wblk + lone), (wblk, (where + 2) * wblk)
 
-    def gate_and_up(which, expert):
+    def half_of(part):
+        return pl.ds(part * half, half)
+
+    def groups_of(part):
+        return range(part * GROUPS // HALVES, (part + 1) * GROUPS // HALVES)
+
+    def gate_and_up(which, part, expert):
+        here = half_of(part)
+
         def multiply(where, offset, row, size, first=False):
             offset, row = pl.multiple_of(offset, 128), pl.multiple_of(row, 128)
             for g in range(2):
-                part = dot(
-                    recv_k[which, where, :, pl.ds(offset, size)], wi[expert, g, pl.ds(row, size), :]
+                term = dot(
+                    recv_k[which, where, here, pl.ds(offset, size)],
+                    wi[expert, g, pl.ds(row, size), :],
                 )
                 if first:
-                    acc[g] = part
+                    acc[g, here, :] = term
                 else:
-                    acc[g] += part
+                    acc[g, here, :] += term
 
         def multiply_alone(where, chip, first=False):
             multiply(where, *alone_at(where, chip), lone, first)
@@ -414,18 +428,18 @@
         else:
             multiply(core, 0, core * wblk, wblk, True)
             multiply(core, wblk, (core + 2) * wblk, wblk)
-        for g in range(GROUPS):
+        for g in groups_of(part):
             forward_near(which, g).wait_recv()
         if which == 0:
             multiply_alone(1 - core, x_lo)
             multiply_common(1 - core)
-            for g in range(GROUPS):
+            for g in groups_of(part):
                 forward_far(which, g).wait_recv()
             multiply_alone(1 - core, 1 - x_lo)
         else:
             multiply(1 - core, 0, (1 - core) * wblk, wblk)
             multiply(1 - core, wblk, (3 - core) * wblk, wblk)
-        hid[...] = gated(acc[0], acc[1])
+        hid[here, :] = gated(acc[0, here, :], acc[1, here, :])
 
     def tiles_at(where):
         return (
@@ -434,17 +448,29 @@
             *((*place, common) for place in common_at(where)),
         )
 
-    def give_tile(which, t):
+    def give_tile(which, part, t):
         offset, _, size = tiles_at(core)[t]
-        span = pl.ds(pl.multiple_of(offset, 128), size)
-        return give(which, t, recv_k.at[which, 1 - core], in_k.at[which], span)
-
-    def cross(which):
+        here = half_of(part)
+        return give(
+            which,
+            part,
+            t,
+            recv_k.at[which, 1 - core, here],
+            in_k.at[which, here],
+            pl.ds(pl.multiple_of(offset, 128), size),
+        )
+
+    def cross(which, part):
+        here = half_of(part)
         return remote(
-            recv_k.at[which, core, :, far], in_x.at[which], xsend.at[which], xrecv.at[which], mate
+            recv_k.at[which, core, here, far],
+            in_x.at[which, here],
+            xsend.at[which, part],
+            xrecv.at[which, part],
+            mate,
         )
 
-    def send_back(which, kind, columns):
+    def send_back(which, part, kind, columns):
         slot = ret.at[pl.ds(pl.multiple_of(kind * per_kind + pair * CAP, CAP), CAP), columns]
 
         def back(i, carry):
@@ -457,13 +483,16 @@
             ).start()
             return carry
 
-        lax.fori_loop(1, nwide, back, 0)
-        pltpu.make_async_copy(
-            block(recv_k.at[which, core], 0).at[:, columns], slot, rrecv.at[kind]
-        ).start()
-
-    def down(which, expert, kind):
-        for g in range(GROUPS):
+        each = nwide // HALVES
+        lax.fori_loop(max(1, part * each), (part + 1) * each, back, 0)
+        if part == 0:
+            pltpu.make_async_copy(
+                block(recv_k.at[which, core], 0).at[:, columns], slot, rrecv.at[kind]
+            ).start()
+
+    def down(which, part, expert, kind):
+        here = half_of(part)
+        for g in groups_of(part):
             forward_near(which, g).wait_send()
             if which == 0:
                 lend(which, g).wait_send()
@@ -471,65 +500,88 @@
         for t, (offset, column, size) in enumerate(tiles_at(1 - core)):
             span = pl.ds(pl.multiple_of(offset, 128), size)
             columns = pl.ds(pl.multiple_of(column, 128), size)
-            recv_k[which, 1 - core, :, span] = dot(hid[...], wd[expert, :, columns]).astype(BF16)
-            give_tile(which, t).start()
+            recv_k[which, 1 - core, here, span] = dot(
+                hid[here, :], wd[expert, :, columns]
+            ).astype(BF16)
+            give_tile(which, part, t).start()
 
         def own_tile(t):
             offset, column, size = tiles_at(core)[t]
             span = pl.ds(pl.multiple_of(offset, 128), size)
             columns = pl.ds(pl.multiple_of(column, 128), size)
-            give_tile(which, t).wait_recv()
-            recv_k[which, core, :, span] = (
-                dot(hid[...], wd[expert, :, columns]) + in_k[which, :, span].astype(F32)
+            give_tile(which, part, t).wait_recv()
+            recv_k[which, core, here, span] = (
+                dot(hid[here, :], wd[expert, :, columns]) + in_k[which, here, span].astype(F32)
             ).astype(BF16)
 
         own_tile(0)
-        cross(which).start()
+        cross(which, part).start()
         own_tile(2)
         own_tile(3)
-        send_back(which, kind, pl.ds(lone, 2 * common))
+        send_back(which, part, kind, pl.ds(lone, 2 * common))
         own_tile(1)
 
-    def finish(which, kind):
-        cross(which).wait_recv()
+    def finish(which, part, kind):
+        here = half_of(part)
+        cross(which, part).wait_recv()
         lot = alone(x_lo)
-        recv_k[which, core, :, lot] = (
-            recv_k[which, core, :, lot].astype(F32) + in_x[which].astype(F32)
+        recv_k[which, core, here, lot] = (
+            recv_k[which, core, here, lot].astype(F32) + in_x[which, here].astype(F32)
         ).astype(BF16)
-        send_back(which, kind, lot)
-        cross(which).wait_send()
-        for t in range(4):
-            give_tile(which, t).wait_send()
+        send_back(which, part, kind, lot)
+
+    def settle(which):
+        for part in range(HALVES):
+            cross(which, part).wait_send()
+            for t in range(4):
+                give_tile(which, part, t).wait_send()
 
     first_expert = owner * unchanged
-    for g in range(GROUPS + 1):
+    first_kind = owner * 2
+    for g in range(GROUPS):
         relay(0, g)
+        if g > 0:
+            relay_far(0, g - 1)
     loads[4].wait()
     loads[5].wait()
-    gate_and_up(0, first_expert)
-    down(0, first_expert, owner * 2)
+    gate_and_up(0, 0, first_expert)
+    relay_far(0, GROUPS - 1)
+    down(0, 0, first_expert, first_kind)
+    gate_and_up(0, 1, first_expert)
+    down(0, 1, first_expert, first_kind)
     fresh_partial()
+    finish(0, 0, first_kind)
 
     @pl.when(owner == 0)
     def _():
         relay(1, 0)
         relay(1, 1)
 
-    finish(0, owner * 2)
+    finish(0, 1, first_kind)
 
     @pl.when(owner == 0)
     def _():
+        gate_and_up(1, 0, 1)
+        down(1, 0, 1, 1)
         for g in range(2, GROUPS):
             relay(1, g)
-        gate_and_up(1, 1)
-        down(1, 1, 1)
+        gate_and_up(1, 1, 1)
+        down(1, 1, 1, 1)
 
     fresh_hidden()
-    fresh_down_and_back()
 
     @pl.when(owner == 0)
     def _():
-        finish(1, 1)
+        finish(1, 0, 1)
+
+    fresh_down_and_back()
+
+    @pl.when(owner == 0)
+    def _():
+        finish(1, 1, 1)
+        settle(1)
+
+    settle(0)
 
     for kind in (0, 2, 3, 1):
         span = pl.ds(kind * per_kind, per_kind)
@@ -602,7 +654,7 @@
             pltpu.VMEM((2, total // 2, units), F32),
             pltpu.VMEM((total, wblk), BF16),
             pltpu.VMEM((2, total, 2 * wblk), BF16),
-            pltpu.VMEM((2, total, wblk * 3 // 4), BF16),
+            pltpu.VMEM((2, total, wblk * 7 // 8), BF16),
             pltpu.VMEM((slots, 2 * wblk), BF16),
             pltpu.VMEM((2, rows, wblk), F32),
             pltpu.VMEM((rows, wblk), BF16),
@@ -614,10 +666,10 @@
             dma((3, GROUPS, 2)),
             dma((2, GROUPS)),
             dma((2, GROUPS)),
-            dma((2,)),
-            dma((2,)),
-            dma((3, 4)),
-            dma((3, 4)),
+            dma((2, HALVES)),
+            dma((2, HALVES)),
+            dma((3, HALVES, 4)),
+            dma((3, HALVES, 4)),
             dma((3,)),
             dma((3,)),
             dma((3,)),

time: 123 us -> 117 us (0.951)
  Pallas kernels: 121 us -> 116 us
    pallas_call x1, Pallas kernels: 121 us -> 116 us  [on_device(): pl.pallas_call(functools.partial(kernel, nwide), out_shape=jax.ShapeDtype...]
where the time goes in v4:
time: 117 us
  Pallas kernels  116 us (99%)
  local copies, waits for them, and re-layouts  1.62 us (1%)
    pallas_call x1, Pallas kernels, on_device(): pl.pallas_call(functools.partial(kernel, nwide), out_shape=jax.ShapeDtype...  116 us

profile of v4, /device:TPU:1, one launch (start us, length us, event | category | flops | bytes accessed | tf_op | source)
XLA Modules:
  0.0 117.2 jit_solution(6399155143154798863)
XLA Ops:
  0.0 115.6 %shard_map.82 = bf16[96,1024]{1,0:T(8,128)(2,1)} custom-call(bf16[96,4096]{1,0:T(8,128)(2,1)} %tok_hbm.1, s32[8,96]{1,0:T(8,128)} %bitcast.2, f32[8,96]{1,0:T(8,128)} %bitcast.3, s32[16]{0:T(128)} %slot_ref.1, bf16[2,2,4096,384]{3,2,1,0:T(8,128)(2,1)} %wi_hbm.1, bf16[2,384,4096]{2,1,0:T(8,128)(2,1)} %wd_hbm.1, bf16[2,2048,384]{2,1,0:T(8,128)(2,1)} %fi_hbm.1, ...), custom_call_target="tpu_custom_call" | custom-call | tf_op jit(solution)/shard_map/pallas_call | solution.py:633
  115.6 1.6 %copy.10 = bf16[96,1024]{1,0:T(8,128)(2,1)} copy(bf16[96,1024]{1,0:T(8,128)(2,1)} %shard_map.82) | data formatting | bytes 393216

commit v5 on v4

--- a/solution.py
+++ b/solution.py
@@ -568,12 +568,11 @@
         gate_and_up(1, 1, 1)
         down(1, 1, 1, 1)
 
-    fresh_hidden()
-
     @pl.when(owner == 0)
     def _():
         finish(1, 0, 1)
 
+    fresh_hidden()
     fresh_down_and_back()
 
     @pl.when(owner == 0)

time: 117 us -> 125 us (1.068); the launches traced: 117 us -> 122 us
  Pallas kernels: 116 us -> 121 us
    pallas_call x1, Pallas kernels: 116 us -> 121 us  [on_device(): pl.pallas_call(functools.partial(kernel, nwide), out_shape=jax.ShapeDtype...]
where the time goes in v5:
time: 125 us; the launch traced here: 122 us
  Pallas kernels  121 us (97%)
  local copies, waits for them, and re-layouts  1.62 us (1%)
    pallas_call x1, Pallas kernels, on_device(): pl.pallas_call(functools.partial(kernel, nwide), out_shape=jax.ShapeDtype...  121 us

profile of v5, /device:TPU:1, one launch (start us, length us, event | category | flops | bytes accessed | tf_op | source)
XLA Modules:
  0.0 122.3 jit_solution(14252722341403396373)
XLA Ops:
  0.0 120.7 %shard_map.82 = bf16[96,1024]{1,0:T(8,128)(2,1)} custom-call(bf16[96,4096]{1,0:T(8,128)(2,1)} %tok_hbm.1, s32[8,96]{1,0:T(8,128)} %bitcast.2, f32[8,96]{1,0:T(8,128)} %bitcast.3, s32[16]{0:T(128)} %slot_ref.1, bf16[2,2,4096,384]{3,2,1,0:T(8,128)(2,1)} %wi_hbm.1, bf16[2,384,4096]{2,1,0:T(8,128)(2,1)} %wd_hbm.1, bf16[2,2048,384]{2,1,0:T(8,128)(2,1)} %fi_hbm.1, ...), custom_call_target="tpu_custom_call" | custom-call | tf_op jit(solution)/shard_map/pallas_call | solution.py:632
  120.7 1.6 %copy.10 = bf16[96,1024]{1,0:T(8,128)(2,1)} copy(bf16[96,1024]{1,0:T(8,128)(2,1)} %shard_map.82) | data formatting | bytes 393216
